TPU v7x, 256 devices: a whole 4x4x8 slice. The times are simulated.
256 devices in a mesh: group: 16 (over z, core), local: 16 (over y, x).
Axes of the slice: x: 4, y: 4, z: 8, core: 2. Of those that a mesh axis runs over, the one named last changes fastest.
Arguments:
- tokens: bfloat16 [16384, 4096], P(('group', 'local')), may hold values from -6 to 6
- segment_ids: int32 [16384, 12], P(('group', 'local')), may hold values from 0 to 255, as said below
- segment_count: int32 [16384], P(('group', 'local')), may hold values from 4 to 12
- gate_values: bfloat16 [16384, 12], P(('group', 'local')), may hold values from 0.099609375 to 1
- gate_weight: bfloat16 [256, 4096, 384], P(('group', 'local')), may hold values from -0.09375 to 0.09375
- up_weight: bfloat16 [256, 4096, 384], P(('group', 'local')), may hold values from -0.09375 to 0.09375
- down_weight: bfloat16 [256, 384, 4096], P(('group', 'local')), may hold values from -0.3125 to 0.3125
Outputs:
- mixed: bfloat16 [16384, 4096], P(('group', 'local'))
Inputs may be any that keep to these rules, and one draw needn't show every extreme that they name: `segment_ids`: segment s is held by device s of the mesh and lies in group s // 16. A token's first segment_count entries are distinct and lie in exactly 4 groups with consecutive numbers modulo 16, one to three segments a group with consecutive local numbers modulo 16, listed group by group; later entries are not used. Of one device's tokens exactly 16 name segments of each group, and at most 3 name any one segment.
All inputs are finite; a program needn't handle non-finite values.
Results may differ from a plain program's by a relative error of at most 0.0064.
Values may be sent and summed in bfloat16 or wider, within the bound.
A program may use at most 128 MiB of HBM per device.

v0:
```python
import functools

import jax
import jax.numpy as jnp
from jax import lax
from jax.experimental import pallas as pl
from jax.experimental.pallas import tpu as pltpu
from jax.sharding import PartitionSpec as P

MESH = pl.DeviceIdType.MESH
F32 = jnp.float32
BF16 = jnp.bfloat16

SETS = 8
ROWS = 16
SLOTS = 3
ORDERS = ((0, 1, 2, 3), (1, 0, 3, 2), (2, 3, 0, 1), (3, 2, 1, 0))


def dot(a, b):
    return jnp.dot(a, b, preferred_element_type=F32)


def dot_nt(a, b):
    return lax.dot_general(a, b, (((1,), (1,)), ((), ())), preferred_element_type=F32)


def iota(shape, dim):
    return lax.broadcasted_iota(jnp.int32, shape, dim)


def flip(value, bits):
    if bits == 1:
        return value + 1 - 2 * lax.rem(value, 2)
    if bits == 2:
        return 3 - value
    if bits == 3:
        return lax.rem(value + 2, 4)
    return value


def moved(local, bits):
    y, x = local // 4, lax.rem(local, 4)
    return flip(y, bits & 3) * 4 + flip(x, bits >> 2)


def one(mask):
    return jnp.where(mask, 1.0, 0.0).astype(BF16)


def kernel(
    groups,
    ids_ref, count_ref, gates_ref, tok_ref, gate_hbm, up_hbm, down_hbm,
    out_ref,
    w_in, w_down, acc, hid,
    take, give, meta_s, meta_r, meta_p, codes, sel, weigh, sel_tmp,
    w_sem, zm_send, zm_recv, pm_send, pm_recv,
    zd_send, zd_recv, zc_send, zc_recv,
    xd_send, xd_recv, xc_send, xc_recv,
    zs, zr, zb, r1, p1, g3, s2, f1,
):
    tokens = tok_ref.shape[0]
    width = hid.shape[1]
    held = groups * ROWS
    pad = groups * SLOTS
    segments = groups * 16
    cols = r1.shape[2]
    set_cols = 4 * cols
    g = lax.axis_index("group")
    l = lax.axis_index("local")

    def rows_of(index):
        return pl.ds(pl.multiple_of(index * ROWS, ROWS), ROWS)

    def columns(index, wide):
        return pl.ds(pl.multiple_of(index * wide, wide), wide)

    def peer(j):
        return lax.rem(g + j, groups)

    barrier = pltpu.get_barrier_semaphore()

    def loop(low, high, step):
        def body(n, carry):
            step(n)
            return carry

        lax.fori_loop(low, high, body, 0)

    loop(1, groups, lambda j: pl.semaphore_signal(barrier, inc=1, device_id=(peer(j), l), device_id_type=MESH))
    for e in range(4):
        pl.semaphore_signal(barrier, inc=1, device_id=(g, moved(l, 1 << e)), device_id_type=MESH)

    weights = [
        pltpu.make_async_copy(gate_hbm.at[0], w_in.at[:, 0:width], w_sem.at[0]),
        pltpu.make_async_copy(up_hbm.at[0], w_in.at[:, width : 2 * width], w_sem.at[1]),
        pltpu.make_async_copy(down_hbm.at[0], w_down, w_sem.at[2]),
    ]
    for copy in weights:
        copy.start()

    ids = jnp.where(iota(ids_ref.shape, 0) < count_ref[...], ids_ref[...], -1)
    gates = gates_ref[...].astype(F32)
    label = iota((segments, tokens), 0)
    seg_gate = jnp.zeros((segments, tokens), F32)
    for k in range(ids.shape[0]):
        seg_gate += jnp.where(ids[k : k + 1] == label, gates[k : k + 1], 0.0)
    is_named = seg_gate > 0
    named = one(is_named)
    in_group = one(iota((segments, 128), 0) // 16 == iota((segments, 128), 1))
    in_group_t = one(iota((128, segments), 0) == iota((128, segments), 1) // 16)
    earlier = one(iota((tokens, tokens), 0) < iota((tokens, tokens), 1))
    visit = dot(in_group_t, named) > 0
    place = jnp.where(visit, dot(one(visit), earlier), -1.0)
    take[...] = one(dot(in_group, place.astype(BF16)) == (iota((held, tokens), 0) % ROWS).astype(F32))
    rank = jnp.where(is_named, dot(named, earlier) + 1.0, 0.0).astype(BF16)
    own_group = iota((held, segments), 0) // ROWS == iota((held, segments), 1) // 16
    fold = one(iota((segments, 128), 0) % 16 == iota((segments, 128), 1))
    fold_far = one(iota((segments, 128), 0) % 16 + 16 == iota((segments, 128), 1))
    ranks = jnp.where(own_group, dot_nt(take[...], rank), 0.0).astype(BF16)
    row_gates = jnp.where(own_group, dot_nt(take[...], seg_gate.astype(BF16)), 0.0).astype(BF16)
    meta_s[...] = (dot(ranks, fold) + dot(row_gates, fold_far)).astype(BF16)

    def gather(k):
        zs[k] = dot(take[...], tok_ref[:, columns(k, set_cols)]).astype(BF16)

    loop(0, SETS, gather)
    acc[...] = jnp.zeros_like(acc)
    eye = one(iota((128, 128), 0) == iota((128, 128), 1))
    eye_held = one(iota((held, held), 0) == iota((held, held), 1))
    eye_tokens = one(iota((tokens, tokens), 0) == iota((tokens, tokens), 1))
    give[...] = dot_nt(eye_tokens, take[...]).astype(BF16)
    meta_r[rows_of(g), :] = meta_s[rows_of(g), :]
    for copy in weights:
        copy.wait()
    pl.semaphore_wait(barrier, groups - 1 + 4)

    def meta_copy(j):
        return pltpu.make_async_remote_copy(
            src_ref=meta_s.at[rows_of(peer(j))], dst_ref=meta_r.at[rows_of(g)],
            send_sem=zm_send, recv_sem=zm_recv,
            device_id=(peer(j), l), device_id_type=MESH,
        )

    def out_copy(k, j):
        return pltpu.make_async_remote_copy(
            src_ref=zs.at[k, rows_of(peer(j)), :], dst_ref=zr.at[k, rows_of(g), :],
            send_sem=zd_send.at[k], recv_sem=zd_recv.at[k],
            device_id=(peer(j), l), device_id_type=MESH,
        )

    def back_copy(k, j):
        return pltpu.make_async_remote_copy(
            src_ref=zr.at[k, rows_of(peer(j)), :], dst_ref=zb.at[k, rows_of(g), :],
            send_sem=zc_send.at[k], recv_sem=zc_recv.at[k],
            device_id=(peer(j), l), device_id_type=MESH,
        )

    def start_all(make):
        loop(1, groups, lambda j: make(j).start())

    def settle(like, send, recv):
        pltpu.make_async_remote_copy(
            src_ref=like, dst_ref=like, send_sem=send, recv_sem=recv,
            device_id=(peer(1), l), device_id_type=MESH,
        ).wait()

    others = held - ROWS

    def start_out(k):
        start_all(functools.partial(out_copy, k))

    def exchange(e, src, dst, send, recv):
        return pltpu.make_async_remote_copy(
            src_ref=src, dst_ref=dst, send_sem=send, recv_sem=recv,
            device_id=(g, moved(l, 1 << e)), device_id_type=MESH,
        )

    def forth(k, v, step):
        i = k * 4 + v
        src, dst = (
            (zr.at[k, :, v * cols : (v + 1) * cols], r1.at[i]),
            (s2.at[i], g3.at[i, 0:2, :, 1]),
            (g3.at[i, 0], g3.at[i, 2]),
            (g3.at[i, 1:3, 1], f1.at[i]),
        )[step]
        return exchange(ORDERS[v][step], src, dst, xd_send.at[step, k], xd_recv.at[step, k])

    def back(k, v, step):
        i = k * 4 + v
        src, dst = (
            (r1.at[i], p1.at[i]),
            (g3.at[i, 0:2, :, 1], s2.at[i]),
            (g3.at[i, 2], g3.at[i, 0]),
            (f1.at[i], g3.at[i, 1:3, 1]),
        )[step]
        return exchange(ORDERS[v][step], src, dst, xc_send.at[step, k], xc_recv.at[step, k])

    def four(k, step):
        return (r1 if step == 0 else s2).at[pl.ds(k * 4, 4)]

    def forth_wait(k, step):
        settle(four(k, step), xd_send.at[step, k], xd_recv.at[step, k])

    def back_wait(k, step):
        settle(four(k, step), xc_send.at[step, k], xc_recv.at[step, k])

    def partner_meta(e):
        return exchange(e, meta_r, meta_p.at[e], pm_send.at[e], pm_recv.at[e])

    start_all(meta_copy)
    start_out(0)
    start_out(1)
    settle(meta_r.at[0:others], zm_send, zm_recv)
    for e in range(4):
        partner_meta(e).start()

    first = (iota((16, held), 1) // ROWS * SLOTS - 1).astype(F32)
    slot = iota((pad, held), 0).astype(F32)

    def decode(index, meta):
        turned = dot_nt(eye, meta)
        codes[index, 0:16] = jnp.where(turned[0:16] > 0, first + turned[0:16], -1.0)
        codes[index, 16:32] = turned[16:32]

    def hits(v, r):
        e1, e2, e3, e4 = ORDERS[v]
        index = 1 + e1 if r else 0
        for b in range(8):
            d2, q, d4 = b >> 2, b >> 1 & 1, b & 1
            segment = moved(l, d2 << e2 | (1 - q) << e3 | d4 << e4)
            hit = slot == codes[index, pl.ds(segment, 1), :]
            yield slice(b * pad, (b + 1) * pad), hit, codes[index, pl.ds(segment + 16, 1), :]

    def build_sel(v, r):
        for at, hit, _ in hits(v, r):
            sel[v, r, at, :] = one(hit)

    def build_weigh(v, r):
        for at, hit, gate in hits(v, r):
            sel_tmp[at, :] = jnp.where(hit, gate, 0.0).astype(BF16)
        weigh[v, r] = dot_nt(eye_held, sel_tmp[...]).astype(BF16)

    decode(0, meta_r[...])
    for v in range(4):
        build_sel(v, 0)

    def partners():
        for e in range(4):
            partner_meta(e).wait()
            decode(1 + e, meta_p[e])
        for v in range(4):
            build_sel(v, 1)

    def select(k, v, r, rows):
        i = k * 4 + v
        chosen = dot(sel[v, r], rows).astype(BF16)
        inner = slice(r * pad, (r + 1) * pad)
        for b in range(4):
            q, d4 = b >> 1, b & 1
            s2[i, q, d4, inner, :] = chosen[(4 + b) * pad : (5 + b) * pad]
            g3[i, q, d4, 0, inner, :] = chosen[b * pad : (b + 1) * pad]

    def block_of(v, r4, b):
        e1, e2, e3, e4 = ORDERS[v]
        return r4 << e4 | (b >> 2) << e3 | (b >> 1 & 1) << e2 | (b & 1) << e1

    def accumulate(k, v, r4, rows):
        part = dot(rows.reshape(8 * pad, cols), w_in[columns(k * 4 + v, cols), :])
        for b in range(8):
            acc[block_of(v, r4, b)] += part[b * pad : (b + 1) * pad]

    def forth_0(k):
        zr[k, rows_of(g), :] = zs[k, rows_of(g), :]
        settle(zr.at[k, 0:others], zd_send.at[k], zd_recv.at[k])
        for v in range(4):
            forth(k, v, 0).start()

        @pl.when(k + 2 < SETS)
        def _():
            start_out(k + 2)

    def forth_own(k):
        for v in range(4):
            select(k, v, 0, zr[k, :, v * cols : (v + 1) * cols])

    def forth_1(k):
        forth_wait(k, 0)
        for v in range(4):
            select(k, v, 1, r1[k * 4 + v])
            forth(k, v, 1).start()

    def forth_2(k):
        forth_wait(k, 1)
        for v in range(4):
            forth(k, v, 2).start()

    def forth_3(k):
        forth_wait(k, 2)
        for v in range(4):
            forth(k, v, 3).start()

    def forth_near(k):
        for v in range(4):
            accumulate(k, v, 0, g3[k * 4 + v, 1:3, 0])

    def forth_far(k):
        forth_wait(k, 3)
        for v in range(4):
            accumulate(k, v, 1, f1[k * 4 + v])

    def back_3(k):
        for v in range(4):
            i = k * 4 + v
            result = dot(hid[...], w_down[:, columns(i, cols)]).astype(BF16)
            for r4 in (1, 0):
                for b in range(8):
                    r3, r2, r1_ = b >> 2, b >> 1 & 1, b & 1
                    inner = slice(r1_ * pad, (r1_ + 1) * pad)
                    c = block_of(v, r4, b)
                    if r4:
                        f1[i, r3, r2, inner, :] = result[c * pad : (c + 1) * pad]
                    else:
                        g3[i, 1 + r3, 0, r2, inner, :] = result[c * pad : (c + 1) * pad]
                if r4:
                    back(k, v, 3).start()

    def back_2(k):
        back_wait(k, 3)
        for v in range(4):
            back(k, v, 2).start()

    def back_1(k):
        back_wait(k, 2)
        for v in range(4):
            back(k, v, 1).start()

    def part_sum(k, v, r):
        i = k * 4 + v
        inner = slice(r * pad, (r + 1) * pad)
        near = g3[i, 0:2, :, 0, inner, :].reshape(4 * pad, cols)
        far = s2[i, :, :, inner, :].reshape(4 * pad, cols)
        return dot(weigh[v, r], jnp.concatenate([near, far], axis=0))

    def back_0(k):
        back_wait(k, 1)
        for v in range(4):
            r1[k * 4 + v] = part_sum(k, v, 1).astype(BF16)
            back(k, v, 0).start()

    def back_own(k):
        back_wait(k, 0)
        for v in range(4):
            own = part_sum(k, v, 0)
            zr[k, :, v * cols : (v + 1) * cols] = (own + p1[k * 4 + v].astype(F32)).astype(BF16)
        start_all(functools.partial(back_copy, k))
        zb[k, rows_of(g), :] = zr[k, rows_of(g), :]

    def back_out(k):
        settle(zb.at[k, 0:others], zc_send.at[k], zc_recv.at[k])
        out_ref[:, columns(k, set_cols)] = dot(give[...], zb[k]).astype(BF16)

    def staggered(stages, once):
        depth = 1 + max(lag for lag, _ in stages)

        def slot_step(t):
            for lag, stage in stages:
                k = t - lag

                @pl.when((k >= 0) & (k < SETS))
                def _(stage=stage, k=k):
                    stage(k)

            for at, extra in once:
                pl.when(t == at)(extra)

        loop(0, SETS + depth - 1, slot_step)

    def weights_back():
        for v in range(4):
            for r in range(2):
                build_weigh(v, r)

    staggered(
        ((4, forth_far), (3, forth_3), (2, forth_2), (1, forth_1), (0, forth_0), (0, forth_own), (3, forth_near)),
        ((0, partners), (3, weights_back)),
    )
    for c in range(16):
        gated = acc[c, :, 0:width]
        upward = acc[c, :, width : 2 * width]
        hid[c * pad : (c + 1) * pad, :] = (gated / (1.0 + jnp.exp(-gated)) * upward).astype(BF16)
    staggered(((0, back_3), (1, back_2), (2, back_1), (3, back_0), (4, back_own), (6, back_out)), ())


def on_device(tokens, segment_ids, segment_count, gate_values, gate_weight, up_weight, down_weight):
    groups = lax.axis_size("group")
    model = tokens.shape[1]
    width = gate_weight.shape[2]
    held = groups * ROWS
    pad = groups * SLOTS
    cols = model // (4 * SETS)
    vmem = pl.BlockSpec(memory_space=pltpu.VMEM)
    hbm = pl.BlockSpec(memory_space=pl.ANY)
    dma = pltpu.SemaphoreType.DMA

    def per_set():
        return pltpu.VMEM((SETS, held, 4 * cols), BF16)

    def per_item(*shape):
        return pltpu.VMEM((SETS * 4,) + shape + (cols,), BF16)

    return pl.pallas_call(
        functools.partial(kernel, groups),
        out_shape=jax.ShapeDtypeStruct(tokens.shape, BF16),
        in_specs=[vmem, vmem, vmem, vmem, hbm, hbm, hbm],
        out_specs=vmem,
        scratch_shapes=[
            pltpu.VMEM((model, 2 * width), BF16),
            pltpu.VMEM((width, model), BF16),
            pltpu.VMEM((16, pad, 2 * width), F32),
            pltpu.VMEM((16 * pad, width), BF16),
            pltpu.VMEM((held, tokens.shape[0]), BF16),
            pltpu.VMEM((tokens.shape[0], held), BF16),
            pltpu.VMEM((held, 128), BF16),
            pltpu.VMEM((held, 128), BF16),
            pltpu.VMEM((4, held, 128), BF16),
            pltpu.VMEM((5, 32, held), F32),
            pltpu.VMEM((4, 2, 8 * pad, held), BF16),
            pltpu.VMEM((4, 2, held, 8 * pad), BF16),
            pltpu.VMEM((8 * pad, held), BF16),
            dma((3,)),
            dma, dma, dma((4,)), dma((4,)),
            *[dma((SETS,))] * 4,
            *[dma((4, SETS))] * 4,
            per_set(), per_set(), per_set(),
            per_item(held), per_item(held),
            per_item(3, 2, 2, 2 * pad),
            per_item(2, 2, 2 * pad), per_item(2, 2, 2 * pad),
        ],
        compiler_params=pltpu.CompilerParams(
            collective_id=0, has_side_effects=True, vmem_limit_bytes=56 * 1024 * 1024
        ),
    )(segment_ids.T, segment_count[None, :], gate_values.T, tokens, gate_weight, up_weight, down_weight)


def solution(mesh):
    return jax.shard_map(
        on_device,
        mesh=mesh,
        in_specs=(
            P(("group", "local"), None),
            P(("group", "local"), None),
            P(("group", "local")),
            P(("group", "local"), None),
            P(("group", "local"), None, None),
            P(("group", "local"), None, None),
            P(("group", "local"), None, None),
        ),
        out_specs=P(("group", "local"), None),
        check_vma=False,
    )
```

profile of v0, /device:TPU:1, one launch (start us, length us, event | category | flops | bytes accessed | tf_op | source)
XLA Modules:
  0.0 179.4 jit_solution(3655422591580272933)
XLA Ops:
  0.0 177.6 %shard_map.73 = bf16[64,4096]{1,0:T(8,128)(2,1)} custom-call(s32[12,64]{1,0:T(8,128)} %bitcast.3, s32[1,64]{1,0:T(1,128)} %bitcast.5, bf16[12,64]{1,0:T(8,128)(2,1)} %bitcast.4, bf16[64,4096]{1,0:T(8,128)(2,1)} %tok_ref.1, bf16[1,4096,384]{2,1,0:T(8,128)(2,1)} %gate_hbm.1, bf16[1,4096,384]{2,1,0:T(8,128)(2,1)} %up_hbm.1, bf16[1,384,4096]{2,1,0:T(8,128)(2,1)} %down_hbm.1), custom_call_target="tpu_custom_call" | custom-call | tf_op jit(solution)/shard_map/pallas_call | solution.py:412
  177.6 1.9 %copy.9 = bf16[64,4096]{1,0:T(8,128)(2,1)} copy(bf16[64,4096]{1,0:T(8,128)(2,1)} %shard_map.73) | data formatting | bytes 1048576
where the time goes:
time: 180 us; the launch traced here: 179 us
  Pallas kernels  178 us (99%)
  local copies, waits for them, and re-layouts  1.87 us (1%)
    pallas_call x1, Pallas kernels, on_device(): pl.pallas_call(functools.partial(kernel, groups), out_shape=jax.ShapeDtyp...  178 us

commit v1 on v0

--- a/solution.py
+++ b/solution.py
@@ -149,9 +149,9 @@
             device_id=(peer(j), l), device_id_type=MESH,
         )
 
-    def back_copy(k, j):
+    def back_copy(k, n, j):
         return pltpu.make_async_remote_copy(
-            src_ref=zr.at[k, rows_of(peer(j)), :], dst_ref=zb.at[k, rows_of(g), :],
+            src_ref=zr.at[pl.ds(k, n), rows_of(peer(j)), :], dst_ref=zb.at[pl.ds(k, n), rows_of(g), :],
             send_sem=zc_send.at[k], recv_sem=zc_recv.at[k],
             device_id=(peer(j), l), device_id_type=MESH,
         )
@@ -353,12 +353,20 @@
         for v in range(4):
             own = part_sum(k, v, 0)
             zr[k, :, v * cols : (v + 1) * cols] = (own + p1[k * 4 + v].astype(F32)).astype(BF16)
-        start_all(functools.partial(back_copy, k))
         zb[k, rows_of(g), :] = zr[k, rows_of(g), :]
+        paired(k, lambda first, n: start_all(functools.partial(back_copy, first, n)))
+
+    def paired(k, step):
+        pl.when(k >= SETS - 2)(lambda: step(k, 1))
+        pl.when((k < SETS - 2) & (lax.rem(k, 2) == 1))(lambda: step(k - 1, 2))
 
     def back_out(k):
-        settle(zb.at[k, 0:others], zc_send.at[k], zc_recv.at[k])
-        out_ref[:, columns(k, set_cols)] = dot(give[...], zb[k]).astype(BF16)
+        def take_in(first, n):
+            settle(zb.at[pl.ds(first, n), 0:others], zc_send.at[first], zc_recv.at[first])
+            for m in range(n):
+                out_ref[:, columns(first + m, set_cols)] = dot(give[...], zb[first + m]).astype(BF16)
+
+        paired(k, take_in)
 
     def staggered(stages, once):
         depth = 1 + max(lag for lag, _ in stages)

time: 180 us -> 184 us (1.022)
  Pallas kernels: 178 us -> 182 us
    pallas_call x1, Pallas kernels: 178 us -> 182 us  [on_device(): pl.pallas_call(functools.partial(kernel, groups), out_shape=jax.ShapeDtyp...]
where the time goes in v1:
time: 184 us
  Pallas kernels  182 us (99%)
  local copies, waits for them, and re-layouts  1.87 us (1%)
    pallas_call x1, Pallas kernels, on_device(): pl.pallas_call(functools.partial(kernel, groups), out_shape=jax.ShapeDtyp...  182 us

profile of v1, /device:TPU:1, one launch (start us, length us, event | category | flops | bytes accessed | tf_op | source)
XLA Modules:
  0.0 184.0 jit_solution(5754735686791509017)
XLA Ops:
  0.0 182.1 %shard_map.73 = bf16[64,4096]{1,0:T(8,128)(2,1)} custom-call(s32[12,64]{1,0:T(8,128)} %bitcast.3, s32[1,64]{1,0:T(1,128)} %bitcast.5, bf16[12,64]{1,0:T(8,128)(2,1)} %bitcast.4, bf16[64,4096]{1,0:T(8,128)(2,1)} %tok_ref.1, bf16[1,4096,384]{2,1,0:T(8,128)(2,1)} %gate_hbm.1, bf16[1,4096,384]{2,1,0:T(8,128)(2,1)} %up_hbm.1, bf16[1,384,4096]{2,1,0:T(8,128)(2,1)} %down_hbm.1), custom_call_target="tpu_custom_call" | custom-call | tf_op jit(solution)/shard_map/pallas_call | solution.py:420
  182.1 1.9 %copy.9 = bf16[64,4096]{1,0:T(8,128)(2,1)} copy(bf16[64,4096]{1,0:T(8,128)(2,1)} %shard_map.73) | data formatting | bytes 1048576

commit v2 on v0

--- a/solution.py
+++ b/solution.py
@@ -124,15 +124,8 @@
     def gather(k):
         zs[k] = dot(take[...], tok_ref[:, columns(k, set_cols)]).astype(BF16)
 
-    loop(0, SETS, gather)
-    acc[...] = jnp.zeros_like(acc)
-    eye = one(iota((128, 128), 0) == iota((128, 128), 1))
-    eye_held = one(iota((held, held), 0) == iota((held, held), 1))
-    eye_tokens = one(iota((tokens, tokens), 0) == iota((tokens, tokens), 1))
-    give[...] = dot_nt(eye_tokens, take[...]).astype(BF16)
-    meta_r[rows_of(g), :] = meta_s[rows_of(g), :]
-    for copy in weights:
-        copy.wait()
+    gather(0)
+    gather(1)
     pl.semaphore_wait(barrier, groups - 1 + 4)
 
     def meta_copy(j):
@@ -211,6 +204,13 @@
     start_all(meta_copy)
     start_out(0)
     start_out(1)
+    loop(2, SETS, gather)
+    acc[...] = jnp.zeros_like(acc)
+    eye = one(iota((128, 128), 0) == iota((128, 128), 1))
+    eye_held = one(iota((held, held), 0) == iota((held, held), 1))
+    eye_tokens = one(iota((tokens, tokens), 0) == iota((tokens, tokens), 1))
+    give[...] = dot_nt(eye_tokens, take[...]).astype(BF16)
+    meta_r[rows_of(g), :] = meta_s[rows_of(g), :]
     settle(meta_r.at[0:others], zm_send, zm_recv)
     for e in range(4):
         partner_meta(e).start()
@@ -376,6 +376,10 @@
 
         loop(0, SETS + depth - 1, slot_step)
 
+    def weights_here():
+        for copy in weights:
+            copy.wait()
+
     def weights_back():
         for v in range(4):
             for r in range(2):
@@ -383,7 +387,7 @@
 
     staggered(
         ((4, forth_far), (3, forth_3), (2, forth_2), (1, forth_1), (0, forth_0), (0, forth_own), (3, forth_near)),
-        ((0, partners), (3, weights_back)),
+        ((0, partners), (2, weights_here), (3, weights_back)),
     )
     for c in range(16):
         gated = acc[c, :, 0:width]

time: 180 us -> 180 us (level)
  no operation moved by 1% of the time
where the time goes in v2:
time: 180 us
  Pallas kernels  178 us (99%)
  local copies, waits for them, and re-layouts  1.87 us (1%)
    pallas_call x1, Pallas kernels, on_device(): pl.pallas_call(functools.partial(kernel, groups), out_shape=jax.ShapeDtyp...  178 us

profile of v2, /device:TPU:1, one launch (start us, length us, event | category | flops | bytes accessed | tf_op | source)
XLA Modules:
  0.0 179.6 jit_solution(2640417101920718417)
XLA Ops:
  0.0 177.8 %shard_map.73 = bf16[64,4096]{1,0:T(8,128)(2,1)} custom-call(s32[12,64]{1,0:T(8,128)} %bitcast.3, s32[1,64]{1,0:T(1,128)} %bitcast.5, bf16[12,64]{1,0:T(8,128)(2,1)} %bitcast.4, bf16[64,4096]{1,0:T(8,128)(2,1)} %tok_ref.1, bf16[1,4096,384]{2,1,0:T(8,128)(2,1)} %gate_hbm.1, bf16[1,4096,384]{2,1,0:T(8,128)(2,1)} %up_hbm.1, bf16[1,384,4096]{2,1,0:T(8,128)(2,1)} %down_hbm.1), custom_call_target="tpu_custom_call" | custom-call | tf_op jit(solution)/shard_map/pallas_call | solution.py:416
  177.8 1.9 %copy.9 = bf16[64,4096]{1,0:T(8,128)(2,1)} copy(bf16[64,4096]{1,0:T(8,128)(2,1)} %shard_map.73) | data formatting | bytes 1048576
